TPU v7x, 128 devices: a whole 4x4x4 slice. The times are simulated.
128 devices in a mesh: cell: 8 (over z_hi, y), blk: 16 (over z_lo, x, core).
Axes of the slice: x: 4, y: 4, z: 4 (z_hi: 2, z_lo: 2; z = z_hi * 2 + z_lo), core: 2. Of those that a mesh axis runs over, the one named last changes fastest.
Arguments:
- codes: bfloat16 [65536, 128], P(('cell', 'blk')), may hold values from -60 to 60
- scales: float32 [65536], P(('cell', 'blk')), may hold values from 0.5 to 2
- coarse_ids: int32 [65536], P(('cell', 'blk')), may hold values from 0 to 7, as said below
- centroids: bfloat16 [131072, 128], P(('cell', 'blk')), may hold values from -6 to 6
Outputs:
- reconstruction: bfloat16 [65536, 128], P(('cell', 'blk'))
- residual: bfloat16 [65536, 128], P(('cell', 'blk'))
Inputs may be any that keep to these rules, and one draw needn't show every extreme that they name: `coarse_ids`: on every device, the number of its 512 rows that name partition g is the same for all devices; at most 128 rows of one device name one partition, and one partition is named by exactly 128 rows of every device.
All inputs are finite; a program needn't handle non-finite values.
Results may differ from a plain program's by a relative error of at most 0.006.
Values may be sent and summed in bfloat16 or wider, within the bound.
A program may use at most 256 MiB of HBM per device.

v0:
```python
import math

import jax
import jax.numpy as jnp
from jax import lax
from jax.sharding import PartitionSpec as P


def local(codes, scales, coarse_ids, centroids):
    rows_dev = codes.shape[0]
    width = codes.shape[1]
    loops = lax.axis_size("cell")
    cap = 2 * rows_dev // loops
    beta = 1.0 / math.sqrt(width)
    dequant = (codes.astype(jnp.float32) * scales[:, None]).astype(jnp.bfloat16)
    onehot = (coarse_ids[:, None] == jnp.arange(loops, dtype=jnp.int32)[None, :]).astype(jnp.int32)
    ranks = jnp.sum(jnp.cumsum(onehot, axis=0) * onehot, axis=1) - 1
    slots = coarse_ids * cap + ranks
    outgoing = jnp.zeros((loops * cap, width), jnp.bfloat16).at[slots].set(dequant)
    arrived = lax.all_to_all(
        outgoing.reshape(loops, cap, width), "cell", split_axis=0, concat_axis=0, tiled=True
    )
    queries = arrived.reshape(loops * cap, width)

    def scores_of(piece):
        product = lax.dot_general(
            queries, piece, (((1,), (1,)), ((), ())), preferred_element_type=jnp.float32
        )
        return product * beta

    top = jnp.max(scores_of(lax.all_gather(centroids, "blk", axis=0, tiled=True)), axis=1)
    piece = lax.all_gather(centroids, "blk", axis=0, tiled=True)
    weights = jnp.exp(scores_of(piece) - top[:, None]).astype(jnp.bfloat16)
    total = jnp.sum(weights.astype(jnp.float32), axis=1)
    numer = jnp.dot(weights, piece, preferred_element_type=jnp.float32)
    total, numer = (total, numer)
    recon = (numer / total[:, None]).astype(jnp.bfloat16)
    remote_residual = (queries.astype(jnp.float32) - recon.astype(jnp.float32)).astype(jnp.bfloat16)
    stacked = jnp.stack([recon, remote_residual]).reshape(2, loops, cap, width)
    back = lax.all_to_all(stacked, "cell", split_axis=1, concat_axis=1, tiled=True).reshape(
        2, loops * cap, width
    )
    return (back[0][slots], back[1][slots])


def solution(mesh):
    in_specs = (
        P(("cell", "blk"), None),
        P(("cell", "blk")),
        P(("cell", "blk")),
        P(("cell", "blk"), None),
    )
    out_specs = (P(("cell", "blk"), None), P(("cell", "blk"), None))
    return jax.shard_map(local, mesh=mesh, in_specs=in_specs, out_specs=out_specs, check_vma=False)
```

profile of v0, /device:TPU:1, one launch (start us, length us, event | category | flops | bytes accessed | tf_op | source)
XLA Modules:
  0.0 157.9 jit_solution(987287009752046674)
XLA Ops:
  7.2 0.0 all-gather.2.cloned.1.call-start
  7.2 0.7 all-gather.2.cloned.1.call-update
  7.9 0.7 fusion.5
  8.6 1.1 reduce-window.6
  9.7 0.2 slice_reduce_fusion
  10.0 0.8 fusion.4
  10.7 0.7 compare_select_fusion
  11.4 2.3 %scatter_custom_fusion = bf16[1024,128]{1,0:T(8,128)(2,1)S(1)} fusion(s32[512]{0:T(512)S(1)} %compare_select_fusion, bf16[512,128]{1,0:T(8,128)(2,1)} %param.4, f32[512]{0:T(512)} %param.5, bf16[]{:T(256)} %constant.8.clone.1), kind=kCustom, calls=%fused_computation.11 | custom fusion | flops 196608 | bytes 395266 | tf_op jit(solution)/shard_map/scatter | solution.py:19
  13.7 15.9 %all_to_all.10 = bf16[8,128,128]{2,1,0:T(8,128)(2,1)S(1)} all-to-all(bf16[8,128,128]{2,1,0:T(8,128)(2,1)S(1)} %bitcast.25), channel_id=1, replica_groups=mesh['cell'=8,'blk'=16] {'cell'}, dimensions={0} | all-to-all | bytes 524288 | tf_op jit(solution)/shard_map/all_to_all | solution.py:20
  29.7 23.5 %all-gather.2.cloned.1.call-done = bf16[16384,128]{1,0:T(8,128)(2,1)} async-done(((bf16[1024,128]{1,0:T(8,128)(2,1)}), bf16[16384,128]{1,0:T(8,128)(2,1)}) %all-gather.2.cloned.1.call-update) | async-done | bytes 4194320 | tf_op jit(solution)/shard_map/all_gather | solution.py:32
  53.1 25.2 %multiply_reduce_fusion = (f32[1024]{0:T(1024)S(1)}, f32[1024,16384]{1,0:T(8,128)}) fusion(bf16[1024,128]{1,0:T(8,128)(2,1)S(1)} %bitcast.24, bf16[16384,128]{1,0:T(8,128)(2,1)} %all-gather.2.cloned.1.call-done), kind=kOutput, calls=%fused_computation.5 | convolution fusion | flops 4328520704 | bytes 71569408 | tf_op jit(solution)/shard_map/dot_general | solution.py:26
  78.4 33.3 %convert_reduce_fusion = (f32[1024]{0:T(1024)S(1)}, bf16[1024,16384]{1,0:T(8,128)(2,1)}) fusion(f32[1024]{0:T(1024)S(1)} %get-tuple-element.6, f32[1024,16384]{1,0:T(8,128)} %get-tuple-element.7), kind=kLoop, calls=%fused_computation.3 | loop fusion | flops 83885056 | bytes 100671488 | tf_op jit(solution)/shard_map/reduce_sum | solution.py:34
  111.7 16.3 %subtract_convert_fusion = (bf16[1024,128]{1,0:T(8,128)(2,1)S(1)}, bf16[1024,128]{1,0:T(8,128)(2,1)S(1)}) fusion(bf16[8,128,128]{2,1,0:T(8,128)(2,1)S(1)} %all_to_all.10, f32[1024]{0:T(1024)S(1)} %get-tuple-element.2, bf16[1024,16384]{1,0:T(8,128)(2,1)} %get-tuple-element.3, bf16[16384,128]{1,0:T(8,128)(2,1)} %all-gather.2.cloned.1.call-done), kind=kOutput, calls=%fused_computation.9 | convolution fusion | flops 4295753728 | bytes 38539264 | tf_op jit(solution)/shard_map/dot_general | solution.py:35
  128.0 0.8 pad_maximum_fusion
  128.9 6.6 %all-to-all-start.1 = ((bf16[2,8,128,128]{3,2,0,1:T(8,128)(2,1)}), bf16[2,8,128,128]{3,2,0,1:T(8,128)(2,1)S(1)}, u32[]{:S(2)}, u32[]{:S(2)}) async-start(bf16[2,8,128,128]{3,2,0,1:T(8,128)(2,1)} %pad_maximum_fusion), calls=%async_computation.1 | async-start | bytes 1048576 | tf_op jit(solution)/shard_map/all_to_all | solution.py:40
  135.5 11.7 %all-to-all-done.1 = bf16[2,8,128,128]{3,2,0,1:T(8,128)(2,1)S(1)} async-done(((bf16[2,8,128,128]{3,2,0,1:T(8,128)(2,1)}), bf16[2,8,128,128]{3,2,0,1:T(8,128)(2,1)S(1)}, u32[]{:S(2)}, u32[]{:S(2)}) %all-to-all-start.1) | async-done | bytes 524320 | tf_op jit(solution)/shard_map/all_to_all | solution.py:40
  147.3 1.9 %gather_fusion.1 = bf16[512,128]{1,0:T(8,128)(2,1)} fusion(bf16[1024,128]{1,0:T(8,128)(2,1)S(1)} %bitcast.23, s32[1024]{0:T(1024)S(1)} %pad_clamp_fusion), kind=kCustom, calls=%fused_computation.1 | custom fusion | bytes 264192 | tf_op jit(solution)/shard_map/gather | solution.py:43
  149.2 1.9 %gather_fusion = bf16[512,128]{1,0:T(8,128)(2,1)} fusion(bf16[1024,128]{1,0:T(8,128)(2,1)S(1)} %bitcast.22, s32[1024]{0:T(1024)S(1)} %pad_clamp_fusion), kind=kCustom, calls=%fused_computation | custom fusion | bytes 264192 | tf_op jit(solution)/shard_map/gather | solution.py:43
  (4 shorter events, 0.1 us)
Async XLA Ops:
  7.2 46.0 %all-gather.2.cloned.1.call-start = ((), (), s32[]{:S(2)}) async-start(), calls=%async_computation.2 | async-start | bytes 4456448 | tf_op jit(solution)/shard_map/all_gather | solution.py:32
  128.9 18.3 %all-to-all-start.1 = ((bf16[2,8,128,128]{3,2,0,1:T(8,128)(2,1)}), bf16[2,8,128,128]{3,2,0,1:T(8,128)(2,1)S(1)}, u32[]{:S(2)}, u32[]{:S(2)}) async-start(bf16[2,8,128,128]{3,2,0,1:T(8,128)(2,1)} %pad_maximum_fusion), calls=%async_computation.1 | async-start | bytes 1048576 | tf_op jit(solution)/shard_map/all_to_all | solution.py:40
Sparse Core Ops, SparseCore 0:
  9.7 43.3 all-gather.1
where the time goes:
time: 158 us
  matrix products  41.6 us (26%)
  other arithmetic  39.8 us (25%)
  waiting for transfers between devices  35.9 us (23%)
  blocking collectives  15.9 us (10%)
  between operations  14.1 us (9%)
  starting transfers between devices  6.63 us (4%)
  local copies, waits for them, and re-layouts  4.09 us (3%)
    reduce_sum x1, other arithmetic, local(): total = jnp.sum(weights.astype(jnp.float32), axis=1)  33.3 us
    dot_general x1, matrix products, scores_of(): lax.dot_general(queries, piece, (((1,), (1,)), ((), ())), preferred_eleme...  25.2 us
    all_gather x1, waiting for transfers between devices, local(): piece = lax.all_gather(centroids, 'blk', axis=0, tiled=True)  23.5 us
    dot_general x1, matrix products, local(): numer = jnp.dot(weights, piece, preferred_element_type=jnp.float32)  16.3 us
    all_to_all x1, blocking collectives, local(): lax.all_to_all(outgoing.reshape(loops, cap, width), 'cell', split_axis=0,...  15.9 us
    all_to_all x1, waiting for transfers between devices, local(): lax.all_to_all(stacked, 'cell', split_axis=1, concat_axis=1, tiled=True)  11.7 us
    all_to_all x1, starting transfers between devices, local(): lax.all_to_all(stacked, 'cell', split_axis=1, concat_axis=1, tiled=True)  6.59 us
    gather x2, local copies, waits for them, and re-layouts, local(): return (back[0][slots], back[1][slots])  3.83 us
  transfers between devices with their start and end apart: 2, of which 2 were waited for; matrix products, arithmetic and copies ran while one was open for 4% of the time, Pallas kernels for 0%

commit v1 on v0

v1 whole, which is shorter than its diff:
```python
import math

import jax
import jax.numpy as jnp
from jax import lax
from jax.experimental import pallas as pl
from jax.experimental.pallas import tpu as pltpu
from jax.sharding import PartitionSpec as P

D = 128
ROWS = 512
CELLS = 8
CAP = 128
SLOTS = CELLS * CAP
HALF = 512
STEP = 4 * HALF
STEPS = 8
RB = 256
NR = SLOTS // RB
SCALE = math.log2(math.e) / math.sqrt(D)
BF = jnp.bfloat16
F32 = jnp.float32
MESH = pl.DeviceIdType.MESH

(O0, O1, A0, B0, Z0, A1, B1, Z1, C0, C1, PA0, PB0, ZC0, ZC1, PA1, PB1) = range(16)


def kernel(codes_ref, scales_ref, ids_ref, cent_ref, recon_ref, resid_ref,
           buf, dequant, perm, qout, qin, qt, top, alpha, acc, ct, sbuf, pbuf, rout, rback,
           own_sem, link_send, link_recv, sib_send, sib_recv, q_send, q_recv, r_send, r_recv):
    cell, blk = lax.axis_index("cell"), lax.axis_index("blk")
    core = lax.rem(blk, 2)
    x = lax.rem(blk // 2, 4)
    z = blk // 8
    right = (cell, z * 8 + lax.rem(x + 1, 4) * 2 + core)
    left = (cell, z * 8 + lax.rem(x + 3, 4) * 2 + core)
    across = (cell, (1 - z) * 8 + x * 2 + core)
    sibling = (cell, z * 8 + x * 2 + 1 - core)

    barrier = pltpu.get_barrier_semaphore()
    for d in range(1, CELLS):
        pl.semaphore_signal(barrier, inc=1, device_id=(lax.rem(cell + d, CELLS), blk), device_id_type=MESH)
    for peer in (right, left, across, sibling):
        pl.semaphore_signal(barrier, inc=1, device_id=peer, device_id_type=MESH)

    def rows_of(unit, c):
        return buf.at[pl.ds(unit * 2 * HALF + c * HALF, HALF), :]

    def link(src, unit, to):
        return pltpu.make_async_remote_copy(
            src_ref=src, dst_ref=rows_of(unit, 0), send_sem=link_send.at[unit], recv_sem=link_recv.at[unit],
            device_id=to, device_id_type=MESH)

    def twin(unit):
        src = cent_ref.at[pl.ds(unit * HALF, HALF), :] if unit in (O0, O1) else rows_of(unit, 0)
        return pltpu.make_async_remote_copy(
            src_ref=src, dst_ref=rows_of(unit, 1), send_sem=sib_send.at[unit], recv_sem=sib_recv.at[unit],
            device_id=sibling, device_id_type=MESH)

    h0 = cent_ref.at[pl.ds(0, HALF), :]
    h1 = cent_ref.at[pl.ds(HALF, HALF), :]
    links = {
        A0: (h0, right), B0: (h0, left), Z0: (h0, across),
        A1: (h1, right), B1: (h1, left), Z1: (h1, across),
        C0: (rows_of(A0, 0), right), C1: (rows_of(B1, 0), left),
        PA0: (rows_of(Z0, 0), right), PB0: (rows_of(Z0, 0), left),
        PA1: (rows_of(Z1, 0), right), PB1: (rows_of(Z1, 0), left),
        ZC0: (rows_of(C0, 0), across), ZC1: (rows_of(C1, 0), across),
    }

    def send(*units):
        for unit in units:
            link(links[unit][0], unit, links[unit][1]).start()

    def arrived(*units):
        for unit in units:
            link(links[unit][0], unit, links[unit][1]).wait_recv()
            twin(unit).start()

    def doubled(*units):
        for unit in units:
            twin(unit).wait_recv()

    own = [pltpu.make_async_copy(cent_ref.at[pl.ds(h * HALF, HALF), :], rows_of(h, 0), own_sem.at[h]) for h in (0, 1)]
    for copy in own:
        copy.start()

    ids = ids_ref[...]
    scales = scales_ref[...]
    for a in range(ROWS // 128):
        rs = slice(a * 128, (a + 1) * 128)
        column = jnp.broadcast_to(scales[:, rs], (128, 128)).T
        dequant[rs, :] = (codes_ref[rs, :].astype(F32) * column).astype(BF)
    onehot = lax.broadcasted_iota(jnp.int32, (CELLS, ROWS), 0) == ids
    before = lax.broadcasted_iota(jnp.int32, (ROWS, ROWS), 0) <= lax.broadcasted_iota(jnp.int32, (ROWS, ROWS), 1)
    counts = jnp.dot(onehot.astype(F32).astype(BF), before.astype(F32).astype(BF), preferred_element_type=F32)
    rank = jnp.sum(jnp.where(onehot, counts, 0.0), axis=0, keepdims=True) - 1.0
    slot = ids * CAP + rank.astype(jnp.int32)
    spread = (lax.broadcasted_iota(jnp.int32, (SLOTS, ROWS), 0) == slot).astype(F32).astype(BF)
    qout[...] = jnp.dot(spread, dequant[...], preferred_element_type=F32).astype(BF)

    pl.semaphore_wait(barrier, CELLS - 1 + 4)
    twin(O0).start()
    twin(O1).start()

    def block(ref, at):
        return ref.at[pl.ds(pl.multiple_of(at * CAP, CAP), CAP), :]

    def queries(d):
        to = lax.rem(cell + d, CELLS)
        return pltpu.make_async_remote_copy(
            src_ref=block(qout, to), dst_ref=block(qin, cell), send_sem=q_send.at[d], recv_sem=q_recv.at[d],
            device_id=(to, blk), device_id_type=MESH)

    def results(d):
        to = lax.rem(cell + d, CELLS)
        return pltpu.make_async_remote_copy(
            src_ref=block(rout, to), dst_ref=block(rback, cell), send_sem=r_send.at[d], recv_sem=r_recv.at[d],
            device_id=(to, blk), device_id_type=MESH)

    for d in range(1, CELLS):
        queries(d).start()
    send(A0, B0, Z0, A1, B1, Z1)
    mine = pl.ds(pl.multiple_of(cell * CAP, CAP), CAP)
    qin[mine, :] = qout[mine, :]

    places = jnp.broadcast_to(slot, (128, ROWS)).T
    for g in range(CELLS):
        hit = places == g * CAP + lax.broadcasted_iota(jnp.int32, (ROWS, CAP), 1)
        perm[:, g * CAP:(g + 1) * CAP] = hit.astype(F32).astype(BF)
    top[...] = jnp.full_like(top, -1e30)
    alpha[...] = jnp.ones_like(alpha)
    acc[...] = jnp.zeros_like(acc)
    sbuf[...] = jnp.full_like(sbuf, -1e30)
    pbuf[...] = jnp.zeros_like(pbuf)
    ct[...] = jnp.zeros_like(ct)
    for d in range(1, CELLS):
        queries(d).wait_recv()
    qt[...] = qin[...].T

    def stage_scores(c, r):
        rs = slice(r * RB, (r + 1) * RB)
        s = jnp.dot(c, qt[:, rs], preferred_element_type=F32) * SCALE
        old = top[:, rs]
        new = jnp.maximum(old, jnp.max(s, axis=0, keepdims=True))
        sbuf[r % 2] = s
        alpha[:, rs] = jnp.exp2(old - new)
        top[:, rs] = new

    def stage_weights(r):
        rs = slice(r * RB, (r + 1) * RB)
        pbuf[r % 2] = jnp.exp2(sbuf[r % 2] - top[0:1, rs]).astype(BF)

    def stage_sums(r, at):
        rs = slice(r * RB, (r + 1) * RB)
        acc[:, rs] = acc[:, rs] * alpha[0:1, rs] + jnp.dot(ct[at], pbuf[r % 2], preferred_element_type=F32)

    def step(i, at):
        c = buf[pl.ds(pl.multiple_of(i * STEP, STEP), STEP), :]
        ct[at, 0:D, :] = c.T
        ct[at, D:, :] = jnp.ones((16, STEP), BF)
        for r in range(NR):
            stage_scores(c, r)
            stage_weights((r - 1) % NR)
            stage_sums((r - 2) % NR, at if r >= 2 else 1 - at)

    def pair(j, _):
        @pl.when(j == 0)
        def _():
            for copy in own:
                copy.wait()
            doubled(O0, O1)

        @pl.when(j == 1)
        def _():
            arrived(A1, B1, Z1)
            send(C1, PA1, PB1)
            doubled(Z0, A1)

        @pl.when(j == 2)
        def _():
            arrived(C1)
            send(ZC1)
            doubled(C0, C1)

        @pl.when(j == 3)
        def _():
            arrived(ZC0, ZC1)
            doubled(ZC0, ZC1)
        step(2 * j, 0)

        @pl.when(j == 0)
        def _():
            arrived(A0, B0, Z0)
            send(C0, PA0, PB0)
            doubled(A0, B0)

        @pl.when(j == 1)
        def _():
            arrived(C0)
            send(ZC0)
            doubled(B1, Z1)

        @pl.when(j == 2)
        def _():
            arrived(PA0, PB0)
            doubled(PA0, PB0)

        @pl.when(j == 3)
        def _():
            arrived(PA1, PB1)
            doubled(PA1, PB1)
        step(2 * j + 1, 1)
        return 0

    lax.fori_loop(0, STEPS // 2, pair, 0)
    stage_weights(NR - 1)
    stage_sums(NR - 2, 1)
    stage_sums(NR - 1, 1)

    rout[...] = (acc[0:D, :] / acc[D:D + 1, :]).T.astype(BF)
    for d in range(1, CELLS):
        results(d).start()
    rback[mine, :] = rout[mine, :]
    for unit in links:
        link(links[unit][0], unit, links[unit][1]).wait_send()
    for unit in range(16):
        twin(unit).wait_send()
    for d in range(1, CELLS):
        queries(d).wait_send()
    for d in range(1, CELLS):
        results(d).wait_recv()
    recon = jnp.dot(perm[...], rback[...], preferred_element_type=F32)
    recon_ref[...] = recon.astype(BF)
    resid_ref[...] = (dequant[...].astype(F32) - recon).astype(BF)
    for d in range(1, CELLS):
        results(d).wait_send()


def local(codes, scales, coarse_ids, centroids):
    vmem = pl.BlockSpec(memory_space=pltpu.VMEM)
    out = jax.ShapeDtypeStruct((ROWS, D), BF)
    dma = pltpu.SemaphoreType.DMA
    return pl.pallas_call(
        kernel,
        out_shape=(out, out),
        in_specs=[vmem, vmem, vmem, pl.BlockSpec(memory_space=pl.ANY)],
        out_specs=(vmem, vmem),
        scratch_shapes=[
            pltpu.VMEM((STEPS * STEP, D), BF),
            pltpu.VMEM((ROWS, D), BF),
            pltpu.VMEM((ROWS, SLOTS), BF),
            pltpu.VMEM((SLOTS, D), BF),
            pltpu.VMEM((SLOTS, D), BF),
            pltpu.VMEM((D, SLOTS), BF),
            pltpu.VMEM((8, SLOTS), F32),
            pltpu.VMEM((8, SLOTS), F32),
            pltpu.VMEM((D + 16, SLOTS), F32),
            pltpu.VMEM((2, D + 16, STEP), BF),
            pltpu.VMEM((2, STEP, RB), F32),
            pltpu.VMEM((2, STEP, RB), BF),
            pltpu.VMEM((SLOTS, D), BF),
            pltpu.VMEM((SLOTS, D), BF),
            dma((2,)), dma((16,)), dma((16,)), dma((16,)), dma((16,)),
            dma((CELLS,)), dma((CELLS,)), dma((CELLS,)), dma((CELLS,)),
        ],
        compiler_params=pltpu.CompilerParams(
            collective_id=0, has_side_effects=True, vmem_limit_bytes=48 * 2**20),
        cost_estimate=pl.CostEstimate(
            flops=4 * SLOTS * STEPS * STEP * D, bytes_accessed=2**20, transcendentals=SLOTS * STEPS * STEP),
        name="reassign",
    )(codes, scales.reshape(1, ROWS), coarse_ids.reshape(1, ROWS), centroids)


def solution(mesh):
    both = P(("cell", "blk"), None)
    flat = P(("cell", "blk"))
    return jax.shard_map(local, mesh=mesh, in_specs=(both, flat, flat, both), out_specs=(both, both), check_vma=False)
```

time: 158 us -> 56 us (0.35)
  Pallas kernels: 0 us -> 50 us
  matrix products: 41.6 us -> 0 us
  other arithmetic: 39.8 us -> 0 us
  waiting for transfers between devices: 35.9 us -> 0 us
  blocking collectives: 15.9 us -> 0 us
  between operations: 14.1 us -> 0.65 us
  starting transfers between devices: 6.63 us -> 0 us
    pallas_call x0 -> x1, Pallas kernels: none -> 50 us  [local(): pl.pallas_call(kernel, out_shape=(out, out), in_specs=[vmem, vmem, vmem,...]
    dot_general x2 -> x0, matrix products: 41.6 us -> none  [the longest x1 25.2 us: scores_of(): lax.dot_general(queries, piece, (((1,), (1,)), ((), ())), preferred_eleme...]
    reduce_sum x2 -> x0, other arithmetic: 34.1 us -> none  [the longest x1 33.3 us: local(): total = jnp.sum(weights.astype(jnp.float32), axis=1)]
    all_gather x1 -> x0, waiting for transfers between devices: 23.5 us -> none  [local(): piece = lax.all_gather(centroids, 'blk', axis=0, tiled=True)]
    all_to_all x1 -> x0, blocking collectives: 15.9 us -> none  [local(): lax.all_to_all(outgoing.reshape(loops, cap, width), 'cell', split_axis=0,...]
    all_to_all x1 -> x0, waiting for transfers between devices: 11.7 us -> none  [local(): lax.all_to_all(stacked, 'cell', split_axis=1, concat_axis=1, tiled=True)]
    all_to_all x1 -> x0, starting transfers between devices: 6.59 us -> none  [local(): lax.all_to_all(stacked, 'cell', split_axis=1, concat_axis=1, tiled=True)]
    unnamed x0 -> x10, local copies, waits for them, and re-layouts: none -> 4.52 us
  transfers between devices with their start and end apart: 2 -> 0, of which waited for: 2 -> 0; matrix products, arithmetic and copies ran while one was open for 4% -> 0% of each run, Pallas kernels for 0% -> 0%
where the time goes in v1:
time: 56 us; the launch traced here: 55.2 us
  Pallas kernels  50 us (89%)
  local copies, waits for them, and re-layouts  4.52 us (8%)
  between operations  0.65 us (1%)
    pallas_call x1, Pallas kernels, local(): pl.pallas_call(kernel, out_shape=(out, out), in_specs=[vmem, vmem, vmem,...  50 us
    unnamed x10, local copies, waits for them, and re-layouts  4.52 us

profile of v1, /device:TPU:1, one launch (start us, length us, event | category | flops | bytes accessed | tf_op | source)
XLA Modules:
  0.0 55.2 jit_solution(5528331191738328806)
XLA Ops:
  0.6 0.0 copy-start.2
  0.6 0.7 %copy-done.2 = f32[512]{0:T(512)S(1)} copy-done((f32[512]{0:T(512)S(1)}, f32[512]{0:T(512)}, u32[]{:S(2)}) %copy-start.2) | copy-done | bytes 2072
  1.3 0.0 copy-start
  1.3 0.9 %copy-done = bf16[1024,128]{1,0:T(8,128)(2,1)S(1)} copy-done((bf16[1024,128]{1,0:T(8,128)(2,1)S(1)}, bf16[1024,128]{1,0:T(8,128)(2,1)}, u32[]{:S(2)}) %copy-start) | copy-done | bytes 262168
  2.3 0.0 copy-start.1
  2.3 0.9 %copy-done.1 = bf16[512,128]{1,0:T(8,128)(2,1)S(1)} copy-done((bf16[512,128]{1,0:T(8,128)(2,1)S(1)}, bf16[512,128]{1,0:T(8,128)(2,1)}, u32[]{:S(2)}) %copy-start.1) | copy-done | bytes 131096
  3.2 0.0 copy-start.3
  3.2 0.7 %copy-done.3 = s32[512]{0:T(512)S(1)} copy-done((s32[512]{0:T(512)S(1)}, s32[512]{0:T(512)}, u32[]{:S(2)}) %copy-start.3) | copy-done | bytes 2072
  3.9 50.0 %reassign.1 = (bf16[512,128]{1,0:T(8,128)(2,1)S(1)}, bf16[512,128]{1,0:T(8,128)(2,1)S(1)}) custom-call(bf16[512,128]{1,0:T(8,128)(2,1)S(1)} %copy-done.1, f32[1,512]{1,0:T(1,128)S(1)} %bitcast.2, s32[1,512]{1,0:T(1,128)S(1)} %bitcast.3, bf16[1024,128]{1,0:T(8,128)(2,1)S(1)} %copy-done), custom_call_target="tpu_custom_call" | custom-call | flops 8589934592 | bytes 1048576 | tf_op jit(solution)/shard_map/reassign/pallas_call | solution.py:244
  53.8 0.7 %copy.8 = bf16[512,128]{1,0:T(8,128)(2,1)} copy(bf16[512,128]{1,0:T(8,128)(2,1)S(1)} %get-tuple-element.4) | data formatting | bytes 262144
  54.5 0.7 %copy.9 = bf16[512,128]{1,0:T(8,128)(2,1)} copy(bf16[512,128]{1,0:T(8,128)(2,1)S(1)} %get-tuple-element.5) | data formatting | bytes 262144
Async XLA Ops:
  0.6 0.7 %copy-start.2 = (f32[512]{0:T(512)S(1)}, f32[512]{0:T(512)}, u32[]{:S(2)}) copy-start(f32[512]{0:T(512)} %param.5) | copy-start | bytes 6148
  1.3 0.9 %copy-start = (bf16[1024,128]{1,0:T(8,128)(2,1)S(1)}, bf16[1024,128]{1,0:T(8,128)(2,1)}, u32[]{:S(2)}) copy-start(bf16[1024,128]{1,0:T(8,128)(2,1)} %cent_ref.1) | copy-start | bytes 786436
  2.3 0.9 %copy-start.1 = (bf16[512,128]{1,0:T(8,128)(2,1)S(1)}, bf16[512,128]{1,0:T(8,128)(2,1)}, u32[]{:S(2)}) copy-start(bf16[512,128]{1,0:T(8,128)(2,1)} %codes_ref.1) | copy-start | bytes 393220
  3.2 0.7 %copy-start.3 = (s32[512]{0:T(512)S(1)}, s32[512]{0:T(512)}, u32[]{:S(2)}) copy-start(s32[512]{0:T(512)} %param.6) | copy-start | bytes 6148

commit v2 on v1

v2 whole, which is shorter than its diff:
```python
import math

import jax
import jax.numpy as jnp
from jax import lax
from jax.experimental import pallas as pl
from jax.experimental.pallas import tpu as pltpu
from jax.sharding import PartitionSpec as P

D = 128
ROWS = 512
CELLS = 8
CAP = 128
SLOTS = CELLS * CAP
HALF = 512
STEP = 4 * HALF
STEPS = 8
RB = 256
NR = SLOTS // RB
SCALE = math.log2(math.e) / math.sqrt(D)
BF = jnp.bfloat16
F32 = jnp.float32
MESH = pl.DeviceIdType.MESH

(O0, O1, A0, B0, Z0, A1, B1, Z1, C0, C1, PA0, PB0, ZC0, ZC1, PA1, PB1) = range(16)


NEAR = ((0, 0), (0, 1), (0, 3), (0, 2), (1, 0), (1, 1), (1, 3), (1, 2))
BACK = (0, 2, 1, 3, 4, 6, 5, 7)


def kernel(codes_hbm, scales_hbm, ids_hbm, cent_ref, recon_ref, resid_ref,
           buf, codes_ref, scales_ref, ids_ref, dequant, perm, qout, qin, qt, top, alpha, acc, ct, sbuf, rout, rback,
           own_sem, in_sem, link_send, link_recv, sib_send, sib_recv, q_send, q_recv, r_send, r_recv):
    cell, blk = lax.axis_index("cell"), lax.axis_index("blk")
    core = lax.rem(blk, 2)
    x = lax.rem(blk // 2, 4)
    z = blk // 8
    right = (cell, z * 8 + lax.rem(x + 1, 4) * 2 + core)
    left = (cell, z * 8 + lax.rem(x + 3, 4) * 2 + core)
    across = (cell, (1 - z) * 8 + x * 2 + core)
    sibling = (cell, z * 8 + x * 2 + 1 - core)

    def cell_at(dz, dy):
        return lax.rem(cell // 4 + dz, 2) * 4 + lax.rem(lax.rem(cell, 4) + dy, 4)

    barrier = pltpu.get_barrier_semaphore()
    for j in range(1, CELLS):
        pl.semaphore_signal(barrier, inc=1, device_id=(cell_at(*NEAR[j]), blk), device_id_type=MESH)
    for peer in (right, left, across, sibling):
        pl.semaphore_signal(barrier, inc=1, device_id=peer, device_id_type=MESH)

    def rows_of(unit, c):
        return buf.at[pl.ds(unit * 2 * HALF + c * HALF, HALF), :]

    def link(src, unit, to):
        return pltpu.make_async_remote_copy(
            src_ref=src, dst_ref=rows_of(unit, 0), send_sem=link_send.at[unit], recv_sem=link_recv.at[unit],
            device_id=to, device_id_type=MESH)

    def twin(unit):
        src = cent_ref.at[pl.ds(unit * HALF, HALF), :] if unit in (O0, O1) else rows_of(unit, 0)
        return pltpu.make_async_remote_copy(
            src_ref=src, dst_ref=rows_of(unit, 1), send_sem=sib_send.at[unit], recv_sem=sib_recv.at[unit],
            device_id=sibling, device_id_type=MESH)

    h0 = cent_ref.at[pl.ds(0, HALF), :]
    h1 = cent_ref.at[pl.ds(HALF, HALF), :]
    links = {
        A0: (h0, right), B0: (h0, left), Z0: (h0, across),
        A1: (h1, right), B1: (h1, left), Z1: (h1, across),
        C0: (rows_of(A0, 0), right), C1: (rows_of(B1, 0), left),
        PA0: (rows_of(Z0, 0), right), PB0: (rows_of(Z0, 0), left),
        PA1: (rows_of(Z1, 0), right), PB1: (rows_of(Z1, 0), left),
        ZC0: (rows_of(C0, 0), across), ZC1: (rows_of(C1, 0), across),
    }

    def send(*units):
        for unit in units:
            link(links[unit][0], unit, links[unit][1]).start()

    def arrived(*units):
        for unit in units:
            link(links[unit][0], unit, links[unit][1]).wait_recv()
            twin(unit).start()

    def doubled(*units):
        for unit in units:
            twin(unit).wait_recv()

    ins = [pltpu.make_async_copy(src, dst, in_sem.at[n]) for n, (src, dst) in enumerate(
        ((ids_hbm, ids_ref), (scales_hbm, scales_ref), (codes_hbm, codes_ref)))]
    own = [pltpu.make_async_copy(cent_ref.at[pl.ds(h * HALF, HALF), :], rows_of(h, 0), own_sem.at[h]) for h in (0, 1)]
    for copy in ins + own:
        copy.start()
    for copy in ins:
        copy.wait()

    ids = ids_ref[...]
    scales = scales_ref[...]
    for a in range(ROWS // 128):
        rs = slice(a * 128, (a + 1) * 128)
        column = jnp.broadcast_to(scales[:, rs], (128, 128)).T
        dequant[rs, :] = (codes_ref[rs, :].astype(F32) * column).astype(BF)
    onehot = lax.broadcasted_iota(jnp.int32, (CELLS, ROWS), 0) == ids
    before = lax.broadcasted_iota(jnp.int32, (ROWS, ROWS), 0) <= lax.broadcasted_iota(jnp.int32, (ROWS, ROWS), 1)
    counts = jnp.dot(onehot.astype(F32).astype(BF), before.astype(F32).astype(BF), preferred_element_type=F32)
    rank = jnp.sum(jnp.where(onehot, counts, 0.0), axis=0, keepdims=True) - 1.0
    slot = ids * CAP + rank.astype(jnp.int32)
    spread = (lax.broadcasted_iota(jnp.int32, (SLOTS, ROWS), 0) == slot).astype(F32).astype(BF)
    qout[...] = jnp.dot(spread, dequant[...], preferred_element_type=F32).astype(BF)

    def block(ref, at):
        return ref.at[pl.ds(pl.multiple_of(at * CAP, CAP), CAP), :]

    def queries(j):
        to = cell_at(*NEAR[j])
        return pltpu.make_async_remote_copy(
            src_ref=block(qout, to), dst_ref=block(qin, BACK[j]), send_sem=q_send.at[j], recv_sem=q_recv.at[BACK[j]],
            device_id=(to, blk), device_id_type=MESH)

    def queries_here(j):
        return pltpu.make_async_remote_copy(
            src_ref=block(qout, j), dst_ref=block(qin, j), send_sem=q_send.at[j], recv_sem=q_recv.at[j],
            device_id=(cell_at(*NEAR[j]), blk), device_id_type=MESH)

    def results(j, dz, dy, back):
        return pltpu.make_async_remote_copy(
            src_ref=block(rout, j), dst_ref=block(rback, cell), send_sem=r_send.at[j], recv_sem=r_recv.at[back],
            device_id=(cell_at(dz, dy), blk), device_id_type=MESH)

    def results_here(j):
        return pltpu.make_async_remote_copy(
            src_ref=block(rout, j), dst_ref=block(rback, cell_at(*NEAR[j])), send_sem=r_send.at[j],
            recv_sem=r_recv.at[j], device_id=(cell_at(*NEAR[j]), blk), device_id_type=MESH)

    pl.semaphore_wait(barrier, CELLS - 1 + 4)
    for j in range(CELLS - 1, 0, -1):
        queries(j).start()
    send(A0, B0, Z0, A1, B1, Z1)
    twin(O0).start()
    twin(O1).start()
    mine = pl.ds(pl.multiple_of(cell * CAP, CAP), CAP)
    qin[0:CAP, :] = qout[mine, :]

    places = jnp.broadcast_to(slot, (128, ROWS)).T
    for g in range(CELLS):
        hit = places == g * CAP + lax.broadcasted_iota(jnp.int32, (ROWS, CAP), 1)
        perm[:, g * CAP:(g + 1) * CAP] = hit.astype(F32).astype(BF)
    top[...] = jnp.full_like(top, -1e30)
    alpha[...] = jnp.ones_like(alpha)
    acc[...] = jnp.zeros_like(acc)
    sbuf[1] = jnp.full((STEP, RB), -1e30, F32)
    ct[...] = jnp.zeros_like(ct)
    for j in range(1, CELLS):
        queries_here(j).wait_recv()
    for r in range(NR):
        scaled = qin[r * RB:(r + 1) * RB, :].astype(F32) * SCALE
        high = scaled.astype(BF)
        qt[r, 0:D, :] = high.T
        qt[r, D:, :] = (scaled - high.astype(F32)).astype(BF).T

    def unit(i, r, at, n, r_was, at_was):
        q = qt[r]
        high = None
        total = None
        for k in range(2):
            ks = slice(k * (STEP // 2), (k + 1) * (STEP // 2))
            c = buf[pl.ds(pl.multiple_of(i * STEP + k * (STEP // 2), STEP // 2), STEP // 2), :]
            s = jnp.dot(jnp.concatenate([c, c], axis=1), q, preferred_element_type=F32)
            sbuf[n % 2, ks, :] = s
            peak = jnp.max(s.reshape(STEP // 16, 8, RB), axis=0)
            high = peak if high is None else jnp.maximum(high, peak)
            w = jnp.exp2(sbuf[(n + 1) % 2, ks, :] - top[r_was, 0:1, :]).astype(BF)
            part = jnp.dot(ct[at_was, :, ks], w, preferred_element_type=F32)
            total = part if total is None else total + part
        acc[r_was] = acc[r_was] * alpha[r_was, 0:1, :] + total
        old = top[r]
        new = jnp.maximum(old, jnp.max(high, axis=0, keepdims=True))
        alpha[r] = jnp.exp2(old - new)
        top[r] = new

    def turn(i, at):
        c = buf[pl.ds(pl.multiple_of(i * STEP, STEP), STEP), :]
        ct[at, 0:D, :] = c.T
        ct[at, D:, :] = jnp.ones((16, STEP), BF)

    def step(i, at):
        turn(i, at)
        for r in range(NR):
            unit(i, r, at, r, (r - 1) % NR, at if r >= 1 else 1 - at)

    def pair(j, _):
        @pl.when(j == 0)
        def _():
            for copy in own:
                copy.wait()
            doubled(O0, O1)

        @pl.when(j == 1)
        def _():
            arrived(A1, B1, Z1)
            send(C1, PA1, PB1)
            doubled(Z0, A1)

        @pl.when(j == 2)
        def _():
            arrived(C1)
            send(ZC1)
            doubled(C0, C1)
        step(2 * j, 0)

        @pl.when(j == 0)
        def _():
            arrived(A0, B0, Z0)
            send(C0, PA0, PB0)
            doubled(A0, B0)

        @pl.when(j == 1)
        def _():
            arrived(C0)
            send(ZC0)
            doubled(B1, Z1)

        @pl.when(j == 2)
        def _():
            arrived(PA0, PB0)
            doubled(PA0, PB0)
        step(2 * j + 1, 1)
        return 0

    lax.fori_loop(0, STEPS // 2 - 1, pair, 0)
    arrived(ZC0, ZC1, PA1, PB1)
    doubled(ZC0, ZC1, PA1, PB1)

    def finish(r):
        rout[pl.ds(pl.multiple_of(r * RB, RB), RB), :] = (acc[r, 0:D, :] / acc[r, D:D + 1, :]).T.astype(BF)

    def last(j, _):
        r = NR - 1 - j
        r_was = jnp.minimum(r + 1, NR - 1)
        turn(STEPS - 2, 0)
        unit(STEPS - 2, r, 0, 0, r_was, 1)
        turn(STEPS - 1, 1)
        unit(STEPS - 1, r, 1, 1, r, 0)
        finish(r_was)

        @pl.when(j > 0)
        def _():
            odd = lax.rem(r_was, 2)
            results(2 * r_was, r_was // 2, 3 * odd, 2 * r_was - odd).start()
            results(2 * r_was + 1, r_was // 2, 1 + odd, 2 * r_was + 2 - odd).start()
        return 0

    lax.fori_loop(0, NR, last, 0)
    w = jnp.exp2(sbuf[1] - top[0, 0:1, :]).astype(BF)
    acc[0] = acc[0] * alpha[0, 0:1, :] + jnp.dot(ct[1], w, preferred_element_type=F32)
    finish(0)
    results(1, 0, 1, BACK[1]).start()
    rback[mine, :] = rout[0:CAP, :]
    for unit_ in links:
        link(links[unit_][0], unit_, links[unit_][1]).wait_send()
    for unit_ in range(16):
        twin(unit_).wait_send()
    for j in range(1, CELLS):
        queries(j).wait_send()
    for j in range(1, CELLS):
        results_here(j).wait_recv()
    recon = jnp.dot(perm[...], rback[...], preferred_element_type=F32)
    recon_ref[...] = recon.astype(BF)
    resid_ref[...] = (dequant[...].astype(F32) - recon).astype(BF)
    for j in range(1, CELLS):
        results_here(j).wait_send()


def local(codes, scales, coarse_ids, centroids):
    vmem = pl.BlockSpec(memory_space=pltpu.VMEM)
    out = jax.ShapeDtypeStruct((ROWS, D), BF)
    dma = pltpu.SemaphoreType.DMA
    return pl.pallas_call(
        kernel,
        out_shape=(out, out),
        in_specs=[pl.BlockSpec(memory_space=pltpu.HBM)] * 4,
        out_specs=(vmem, vmem),
        scratch_shapes=[
            pltpu.VMEM((STEPS * STEP, D), BF),
            pltpu.VMEM((ROWS, D), BF),
            pltpu.VMEM((1, ROWS), F32),
            pltpu.VMEM((1, ROWS), jnp.int32),
            pltpu.VMEM((ROWS, D), BF),
            pltpu.VMEM((ROWS, SLOTS), BF),
            pltpu.VMEM((SLOTS, D), BF),
            pltpu.VMEM((SLOTS, D), BF),
            pltpu.VMEM((NR, 2 * D, RB), BF),
            pltpu.VMEM((NR, 8, RB), F32),
            pltpu.VMEM((NR, 8, RB), F32),
            pltpu.VMEM((NR, D + 16, RB), F32),
            pltpu.VMEM((2, D + 16, STEP), BF),
            pltpu.VMEM((2, STEP, RB), F32),
            pltpu.VMEM((SLOTS, D), BF),
            pltpu.VMEM((SLOTS, D), BF),
            dma((2,)), dma((3,)), dma((16,)), dma((16,)), dma((16,)), dma((16,)),
            dma((CELLS,)), dma((CELLS,)), dma((CELLS,)), dma((CELLS,)),
        ],
        compiler_params=pltpu.CompilerParams(
            collective_id=0, has_side_effects=True, vmem_limit_bytes=60 * 2**20),
        cost_estimate=pl.CostEstimate(
            flops=4 * SLOTS * STEPS * STEP * D, bytes_accessed=2**20, transcendentals=SLOTS * STEPS * STEP),
        name="reassign",
    )(codes, scales.reshape(1, ROWS), coarse_ids.reshape(1, ROWS), centroids)


def solution(mesh):
    both = P(("cell", "blk"), None)
    flat = P(("cell", "blk"))
    return jax.shard_map(local, mesh=mesh, in_specs=(both, flat, flat, both), out_specs=(both, both), check_vma=False)
```

time: 56 us -> 45.4 us (0.81); the launches traced: 55.2 us -> 45.3 us
  Pallas kernels: 50 us -> 42.4 us
  local copies, waits for them, and re-layouts: 4.52 us -> 2.26 us
    pallas_call x1, Pallas kernels: 50 us -> 42.4 us  [local(): pl.pallas_call(kernel, out_shape=(out, out), in_specs=[pl.BlockSpec(memor...]
    unnamed x10 -> x4, local copies, waits for them, and re-layouts: 4.52 us -> 2.26 us
where the time goes in v2:
time: 45.4 us; the launch traced here: 45.3 us
  Pallas kernels  42.4 us (93%)
  local copies, waits for them, and re-layouts  2.26 us (5%)
  between operations  0.65 us (1%)
    pallas_call x1, Pallas kernels, local(): pl.pallas_call(kernel, out_shape=(out, out), in_specs=[pl.BlockSpec(memor...  42.4 us
    unnamed x4, local copies, waits for them, and re-layouts  2.26 us

profile of v2, /device:TPU:1, one launch (start us, length us, event | category | flops | bytes accessed | tf_op | source)
XLA Modules:
  0.0 45.3 jit_solution(11727896064243152647)
XLA Ops:
  0.6 42.4 %reassign.1 = (bf16[512,128]{1,0:T(8,128)(2,1)}, bf16[512,128]{1,0:T(8,128)(2,1)}) custom-call(bf16[512,128]{1,0:T(8,128)(2,1)} %codes_hbm.1, f32[1,512]{1,0:T(1,128)} %bitcast.2, s32[1,512]{1,0:T(1,128)} %bitcast.3, bf16[1024,128]{1,0:T(8,128)(2,1)} %cent_ref.1), custom_call_target="tpu_custom_call" | custom-call | flops 8589934592 | bytes 1048576 | tf_op jit(solution)/shard_map/reassign/pallas_call | solution.py:280
  43.0 0.0 copy-start
  43.0 1.6 %copy.8 = bf16[512,128]{1,0:T(8,128)(2,1)} copy(bf16[512,128]{1,0:T(8,128)(2,1)} %get-tuple-element.4) | data formatting | bytes 262144
  44.6 0.0 copy-done
  44.6 0.7 %copy.9 = bf16[512,128]{1,0:T(8,128)(2,1)} copy(bf16[512,128]{1,0:T(8,128)(2,1)S(1)} %copy-done) | data formatting | bytes 262144
Async XLA Ops:
  43.0 1.6 %copy-start = (bf16[512,128]{1,0:T(8,128)(2,1)S(1)}, bf16[512,128]{1,0:T(8,128)(2,1)}, u32[]{:S(2)}) copy-start(bf16[512,128]{1,0:T(8,128)(2,1)} %get-tuple-element.5) | copy-start | bytes 393220

commit v3 on v2

--- a/solution.py
+++ b/solution.py
@@ -25,6 +25,17 @@
 (O0, O1, A0, B0, Z0, A1, B1, Z1, C0, C1, PA0, PB0, ZC0, ZC1, PA1, PB1) = range(16)
 
 
+ORDER = (
+    (O0, 0), (O1, 0), (O0, 1), (O1, 1),
+    (A0, 0), (B0, 0), (Z0, 0), (A0, 1),
+    (B0, 1), (Z0, 1), (A1, 0), (B1, 0),
+    (A1, 1), (B1, 1), (Z1, 0), (C0, 0),
+    (Z1, 1), (C0, 1), (C1, 0), (PA0, 0),
+    (C1, 1), (PA0, 1), (PB0, 0), (PA1, 0),
+    (PB0, 1), (PA1, 1), (PB1, 0), (ZC0, 0),
+    (PB1, 1), (ZC0, 1), (ZC1, 0), (ZC1, 1),
+)
+
 NEAR = ((0, 0), (0, 1), (0, 3), (0, 2), (1, 0), (1, 1), (1, 3), (1, 2))
 BACK = (0, 2, 1, 3, 4, 6, 5, 7)
 
@@ -51,7 +62,7 @@
         pl.semaphore_signal(barrier, inc=1, device_id=peer, device_id_type=MESH)
 
     def rows_of(unit, c):
-        return buf.at[pl.ds(unit * 2 * HALF + c * HALF, HALF), :]
+        return buf.at[pl.ds(ORDER.index((unit, c)) * HALF, HALF), :]
 
     def link(src, unit, to):
         return pltpu.make_async_remote_copy(
@@ -67,11 +78,11 @@
     h0 = cent_ref.at[pl.ds(0, HALF), :]
     h1 = cent_ref.at[pl.ds(HALF, HALF), :]
     links = {
-        A0: (h0, right), B0: (h0, left), Z0: (h0, across),
-        A1: (h1, right), B1: (h1, left), Z1: (h1, across),
-        C0: (rows_of(A0, 0), right), C1: (rows_of(B1, 0), left),
+        A0: (h0, right), B0: (h1, left), Z0: (h0, across),
+        A1: (h1, right), B1: (h0, left), Z1: (h1, across),
+        C0: (rows_of(A0, 0), right), C1: (rows_of(B0, 0), left),
         PA0: (rows_of(Z0, 0), right), PB0: (rows_of(Z0, 0), left),
-        PA1: (rows_of(Z1, 0), right), PB1: (rows_of(Z1, 0), left),
+        PA1: (rows_of(A1, 0), across), PB1: (rows_of(Z1, 0), left),
         ZC0: (rows_of(C0, 0), across), ZC1: (rows_of(C1, 0), across),
     }
 
@@ -199,39 +210,39 @@
 
         @pl.when(j == 1)
         def _():
-            arrived(A1, B1, Z1)
-            send(C1, PA1, PB1)
-            doubled(Z0, A1)
+            arrived(A1, B1)
+            send(PA1)
+            doubled(B0, Z0)
 
         @pl.when(j == 2)
         def _():
-            arrived(C1)
+            arrived(C1, PA0)
             send(ZC1)
-            doubled(C0, C1)
+            doubled(Z1, C0)
         step(2 * j, 0)
 
         @pl.when(j == 0)
         def _():
             arrived(A0, B0, Z0)
-            send(C0, PA0, PB0)
-            doubled(A0, B0)
+            send(C0, C1, PA0, PB0)
+            doubled(A0)
 
         @pl.when(j == 1)
         def _():
-            arrived(C0)
-            send(ZC0)
-            doubled(B1, Z1)
+            arrived(Z1, C0)
+            send(ZC0, PB1)
+            doubled(A1, B1)
 
         @pl.when(j == 2)
         def _():
-            arrived(PA0, PB0)
-            doubled(PA0, PB0)
+            arrived(PB0, PA1)
+            doubled(C1, PA0)
         step(2 * j + 1, 1)
         return 0
 
     lax.fori_loop(0, STEPS // 2 - 1, pair, 0)
-    arrived(ZC0, ZC1, PA1, PB1)
-    doubled(ZC0, ZC1, PA1, PB1)
+    arrived(PB1, ZC0, ZC1)
+    doubled(PB0, PA1, PB1, ZC0, ZC1)
 
     def finish(r):
         rout[pl.ds(pl.multiple_of(r * RB, RB), RB), :] = (acc[r, 0:D, :] / acc[r, D:D + 1, :]).T.astype(BF)

time: 45.4 us -> 43.1 us (0.949)
  Pallas kernels: 42.4 us -> 40 us
    pallas_call x1, Pallas kernels: 42.4 us -> 40 us  [local(): pl.pallas_call(kernel, out_shape=(out, out), in_specs=[pl.BlockSpec(memor...]
where the time goes in v3:
time: 43.1 us; the launch traced here: 42.9 us
  Pallas kernels  40 us (93%)
  local copies, waits for them, and re-layouts  2.26 us (5%)
  between operations  0.65 us (2%)
    pallas_call x1, Pallas kernels, local(): pl.pallas_call(kernel, out_shape=(out, out), in_specs=[pl.BlockSpec(memor...  40 us
    unnamed x4, local copies, waits for them, and re-layouts  2.26 us

profile of v3, /device:TPU:1, one launch (start us, length us, event | category | flops | bytes accessed | tf_op | source)
XLA Modules:
  0.0 42.9 jit_solution(15520746703242275499)
XLA Ops:
  0.6 40.0 %reassign.1 = (bf16[512,128]{1,0:T(8,128)(2,1)}, bf16[512,128]{1,0:T(8,128)(2,1)}) custom-call(bf16[512,128]{1,0:T(8,128)(2,1)} %codes_hbm.1, f32[1,512]{1,0:T(1,128)} %bitcast.2, s32[1,512]{1,0:T(1,128)} %bitcast.3, bf16[1024,128]{1,0:T(8,128)(2,1)} %cent_ref.1), custom_call_target="tpu_custom_call" | custom-call | flops 8589934592 | bytes 1048576 | tf_op jit(solution)/shard_map/reassign/pallas_call | solution.py:291
  40.7 0.0 copy-start
  40.7 1.6 %copy.8 = bf16[512,128]{1,0:T(8,128)(2,1)} copy(bf16[512,128]{1,0:T(8,128)(2,1)} %get-tuple-element.4) | data formatting | bytes 262144
  42.3 0.0 copy-done
  42.3 0.7 %copy.9 = bf16[512,128]{1,0:T(8,128)(2,1)} copy(bf16[512,128]{1,0:T(8,128)(2,1)S(1)} %copy-done) | data formatting | bytes 262144
Async XLA Ops:
  40.7 1.6 %copy-start = (bf16[512,128]{1,0:T(8,128)(2,1)S(1)}, bf16[512,128]{1,0:T(8,128)(2,1)}, u32[]{:S(2)}) copy-start(bf16[512,128]{1,0:T(8,128)(2,1)} %get-tuple-element.5) | copy-start | bytes 393220
